TPU v7x, 256 devices: a whole 4x4x8 slice. The times are simulated.
256 devices in a mesh: cfg: 2 (over core), pipe: 8 (over z), sp: 16 (over x, y).
Axes of the slice: x: 4, y: 4, z: 8, core: 2. Of those that a mesh axis runs over, the one named last changes fastest.
Arguments:
- hidden: bfloat16 [2, 8, 1024, 5120], P('cfg', 'pipe', 'sp'), may hold values from -1.5 to 1.5
- query: bfloat16 [2, 8, 1024, 4096], P('cfg', 'pipe', 'sp'), may hold values from -16 to 16
- key_new: bfloat16 [2, 8, 1024, 4096], P('cfg', 'pipe', 'sp'), may hold values from -9.6 to 9.6
- value_new: bfloat16 [2, 8, 1024, 4096], P('cfg', 'pipe', 'sp'), may hold values from -6 to 6
- stale_key: bfloat16 [2, 8, 7168, 4096], P('cfg', 'pipe', None, 'sp'), may hold values from -9.5625 to 9.5625
- stale_value: bfloat16 [2, 8, 7168, 4096], P('cfg', 'pipe', None, 'sp'), may hold values from -6 to 6
- out_weight: bfloat16 [8, 4096, 5120], P('pipe', None, 'sp'), may hold values from -0.09375 to 0.09375
Outputs:
- next_input: bfloat16 [2, 8, 1024, 5120], P('cfg', 'pipe', 'sp')
- guided: bfloat16 [8, 1024, 5120], P('pipe', 'sp', 'cfg')
All inputs are finite; a program needn't handle non-finite values.
Results may differ from a plain program's by a relative error of at most 0.014.
Values may be sent and summed in bfloat16 or wider, within the bound.
A program may use at most 128 MiB of HBM per device.

v0:
```python
import jax
import jax.numpy as jnp
from jax import lax
from jax.sharding import PartitionSpec as P

HEAD_DIM = 128


guidance_scale = 5.0


def from_behind(array, axis, by):
    devices = lax.axis_size(axis)
    return lax.ppermute(array, axis, [(i, (i + by) % devices) for i in range(devices)])


def from_partner(array, axis, bit):
    return lax.ppermute(array, axis, [(i, i ^ 1 << bit) for i in range(lax.axis_size(axis))])


def attend(query_rows, key_rows, value_rows):
    count = query_rows.shape[0]
    heads = query_rows.shape[1] // HEAD_DIM
    block = min(512, count)
    scale = 1.0 / HEAD_DIM**0.5
    q_blocks = query_rows.reshape(count // block, block, heads, HEAD_DIM)
    k_heads = key_rows.reshape(-1, heads, HEAD_DIM)
    v_heads = value_rows.reshape(-1, heads, HEAD_DIM)

    def one_block(q_block):
        scores = (
            jnp.einsum("qhd,khd->hqk", q_block, k_heads, preferred_element_type=jnp.float32) * scale
        )
        weights = jnp.exp(scores - jnp.max(scores, axis=-1, keepdims=True))
        total = jnp.sum(weights, axis=-1)
        mixed = jnp.einsum(
            "hqk,khd->qhd",
            weights.astype(jnp.bfloat16),
            v_heads,
            preferred_element_type=jnp.float32,
        )
        mixed = mixed / total.T[:, :, None]
        return mixed.astype(jnp.bfloat16).reshape(block, heads * HEAD_DIM)

    return lax.map(one_block, q_blocks).reshape(count, heads * HEAD_DIM)


def on_device(hidden, query, key_new, value_new, stale_key, stale_value, out_weight):
    q_tokens = query[0, 0]
    k_tokens = key_new[0, 0]
    v_tokens = value_new[0, 0]
    q_all = lax.all_to_all(q_tokens, "sp", split_axis=1, concat_axis=0, tiled=True)
    k_all, v_all = (
        lax.all_to_all(k_tokens, "sp", split_axis=1, concat_axis=0, tiled=True),
        lax.all_to_all(v_tokens, "sp", split_axis=1, concat_axis=0, tiled=True),
    )
    keys = jnp.concatenate([k_all, stale_key[0, 0]], axis=0)
    values = jnp.concatenate([v_all, stale_value[0, 0]], axis=0)
    attended = attend(q_all, keys, values)
    weight = out_weight[0]
    features = lax.all_gather(attended, "sp", axis=1, tiled=True)
    columns = jnp.dot(features, weight, preferred_element_type=jnp.float32)
    projected = lax.all_to_all(
        columns.astype(jnp.bfloat16), "sp", split_axis=0, concat_axis=1, tiled=True
    ).astype(columns.dtype)
    block_out = (hidden[0, 0].astype(jnp.float32) + projected).astype(jnp.bfloat16)
    handed = from_behind(block_out, "pipe", 1)
    half_width = block_out.shape[1] // 2
    mine = lax.axis_index("cfg")
    outgoing = lax.dynamic_slice_in_dim(block_out, (1 - mine) * half_width, half_width, 1)
    own_part = lax.dynamic_slice_in_dim(block_out, mine * half_width, half_width, 1)
    partner = from_partner(outgoing, "cfg", 0)
    is_first = mine == 0
    cond = jnp.where(is_first, own_part, partner).astype(jnp.float32)
    uncond = jnp.where(is_first, partner, own_part).astype(jnp.float32)
    guided = (uncond + guidance_scale * (cond - uncond)).astype(jnp.bfloat16)
    return (handed[None, None], guided[None])


def solution(mesh):
    return jax.shard_map(
        on_device,
        mesh=mesh,
        in_specs=(
            P("cfg", "pipe", "sp", None),
            P("cfg", "pipe", "sp", None),
            P("cfg", "pipe", "sp", None),
            P("cfg", "pipe", "sp", None),
            P("cfg", "pipe", None, "sp"),
            P("cfg", "pipe", None, "sp"),
            P("pipe", None, "sp"),
        ),
        out_specs=(P("cfg", "pipe", "sp", None), P("pipe", "sp", "cfg")),
        check_vma=False,
    )
```

profile of v0, /device:TPU:1, one launch (start us, length us, event | category | flops | bytes accessed | tf_op | source)
XLA Modules:
  0.0 316.5 jit_solution(10964107865838538899)
XLA Ops:
  7.2 1.3 copy.39
  8.5 1.0 copy.24
  9.4 7.6 %all-to-all-start.1 = ((bf16[64,16,256]{2,0,1:T(8,128)(2,1)}), bf16[64,16,256]{2,0,1:T(8,128)(2,1)S(1)}, u32[]{:S(2)}, u32[]{:S(2)}) async-start(bf16[64,16,256]{2,0,1:T(8,128)(2,1)} %copy.24), calls=%async_computation.1 | async-start | bytes 1048576 | tf_op jit(solution)/shard_map/all_to_all | solution.py:54
  17.0 1.1 copy.38
  18.2 1.0 copy.23
  19.1 8.2 %all-to-all-done.1 = bf16[64,16,256]{2,0,1:T(8,128)(2,1)S(1)} async-done(((bf16[64,16,256]{2,0,1:T(8,128)(2,1)}), bf16[64,16,256]{2,0,1:T(8,128)(2,1)S(1)}, u32[]{:S(2)}, u32[]{:S(2)}) %all-to-all-start.1) | async-done | bytes 524320 | tf_op jit(solution)/shard_map/all_to_all | solution.py:54
  27.3 4.2 %all-to-all-start = ((bf16[64,16,256]{2,0,1:T(8,128)(2,1)}), bf16[64,16,256]{2,0,1:T(8,128)(2,1)}, u32[]{:S(2)}, u32[]{:S(2)}) async-start(bf16[64,16,256]{2,0,1:T(8,128)(2,1)} %copy.23), calls=%async_computation | async-start | bytes 1048576 | tf_op jit(solution)/shard_map/all_to_all | solution.py:52
  31.6 6.0 %copy.25 = bf16[1,1,7168,256]{2,3,1,0:T(8,128)(2,1)} copy(bf16[1,1,7168,256]{3,2,1,0:T(8,128)(2,1)} %param.13) | data formatting | bytes 7340032 | tf_op args[4]
  37.6 6.0 %copy.28 = bf16[1,1,7168,256]{2,3,1,0:T(8,128)(2,1)} copy(bf16[1,1,7168,256]{3,2,1,0:T(8,128)(2,1)} %param.14) | data formatting | bytes 7340032 | tf_op args[5]
  43.5 1.1 copy.40
  44.7 1.0 copy.27
  45.6 0.9 concatenate.16
  46.5 1.3 copy.26
  47.9 6.6 %all-to-all-start.2 = ((bf16[64,16,256]{2,0,1:T(8,128)(2,1)}), bf16[64,16,256]{2,0,1:T(8,128)(2,1)}, u32[]{:S(2)}, u32[]{:S(2)}) async-start(bf16[64,16,256]{2,0,1:T(8,128)(2,1)} %copy.27), calls=%async_computation.2 | async-start | bytes 1048576 | tf_op jit(solution)/shard_map/all_to_all | solution.py:55
  54.5 0.2 all-gather.2.cloned.1.call-start
  54.7 4.4 %pad_maximum_fusion = bf16[8192,2,128]{0,2,1:T(8,128)(2,1)} fusion(bf16[7168,2,128]{0,2,1:T(8,128)(2,1)} %bitcast.62, bf16[1024,2,128]{0,2,1:T(8,128)(2,1)S(1)} %copy.26), kind=kLoop, calls=%fused_computation.13 | loop fusion | flops 8388608 | bytes 8388608 | tf_op jit(solution)/shard_map/concatenate | solution.py:57
  59.1 2.0 reshape.44
  61.1 6.4 %copy.31 = bf16[8192,2,128]{2,0,1:T(8,128)(2,1)} copy(bf16[8192,2,128]{0,2,1:T(8,128)(2,1)} %pad_maximum_fusion) | data formatting | bytes 8388608 | tf_op jit(solution)/shard_map/while | solution.py:45
  67.5 2.0 concatenate.19
  69.4 1.3 copy.29
  70.7 4.4 %pad_maximum_fusion.1 = bf16[8192,2,128]{0,2,1:T(8,128)(2,1)} fusion(bf16[7168,2,128]{0,2,1:T(8,128)(2,1)} %bitcast.61, bf16[1024,2,128]{0,2,1:T(8,128)(2,1)S(1)} %copy.29), kind=kLoop, calls=%fused_computation.14 | loop fusion | flops 8388608 | bytes 8388608 | tf_op jit(solution)/shard_map/concatenate | solution.py:58
  75.2 93.1 %while.10 = (s32[]{:T(128)}, bf16[2,512,256]{2,1,0:T(8,128)(2,1)}, bf16[2,512,2,128]{3,2,1,0:T(2,128)(2,1)}, bf16[8192,2,128]{2,0,1:T(8,128)(2,1)}, bf16[8192,2,128]{0,2,1:T(8,128)(2,1)}, /*index=5*/s32[]{:T(128)}) while((s32[]{:T(128)}, bf16[2,512,256]{2,1,0:T(8,128)(2,1)}, bf16[2,512,2,128]{3,2,1,0:T(2,128)(2,1)}, ...), condition=%wide.region_3.4_spmd, body=%wide.region_0.3_spmd.sunk | while | flops 4362336256 | bytes 111169624 | solution.py:45
  75.2 1.1 constant_dynamic-slice_fusion.3
  76.3 15.4 %multiply_reduce_fusion.2 = (f32[2,512]{1,0:T(2,128)S(1)}, f32[2,512,8192]{2,1,0:T(8,128)}) fusion(bf16[8192,2,128]{2,0,1:T(8,128)(2,1)} %get-tuple-element.102, bf16[1,512,2,128]{3,2,1,0:T(2,128)(2,1)S(1)} %constant_dynamic-slice_fusion.3), kind=kOutput, calls=%fused_computation.1.clone.1 | convolution fusion | flops 2164259840 | bytes 38014976 | tf_op jit(solution)/shard_map/while/body/eval_jaxpr/qhd,khd->hqk/dot_general | solution.py:32
  91.7 14.1 %fusion.35 = f32[2,512]{1,0:T(2,128)S(1)} fusion(f32[2,512,8192]{2,1,0:T(8,128)} %get-tuple-element.85, f32[2,512]{1,0:T(2,128)S(1)} %get-tuple-element.86), kind=kLoop, calls=%fused_computation.2.clone.1 | loop fusion | flops 25164800 | bytes 33562624 | tf_op jit(solution)/shard_map/while/body/eval_jaxpr/reduce_sum | solution.py:35
  105.7 15.1 %fusion.36 = bf16[512,2,128]{0,2,1:T(8,128)(2,1)S(1)} fusion(bf16[8192,2,128]{0,2,1:T(8,128)(2,1)} %get-tuple-element.103, f32[2,512,8192]{2,1,0:T(8,128)} %get-tuple-element.85, f32[2,512]{1,0:T(2,128)S(1)} %get-tuple-element.86, f32[512,2]{0,1:T(2,128)S(1)} %bitcast.68), kind=kOutput, calls=%fused_computation.7.clone.1 | convolution fusion | flops 2172911616 | bytes 38019072 | tf_op jit(solution)/shard_map/while/body/eval_jaxpr/hqk,khd->qhd/dot_general | solution.py:36
  121.0 0.7 constant_dynamic-update-slice_fusion.2
  121.7 1.1 constant_dynamic-slice_fusion.3
  122.8 15.4 %multiply_reduce_fusion.2 = (f32[2,512]{1,0:T(2,128)S(1)}, f32[2,512,8192]{2,1,0:T(8,128)}) fusion(bf16[8192,2,128]{2,0,1:T(8,128)(2,1)} %get-tuple-element.102, bf16[1,512,2,128]{3,2,1,0:T(2,128)(2,1)S(1)} %constant_dynamic-slice_fusion.3), kind=kOutput, calls=%fused_computation.1.clone.1 | convolution fusion | flops 2164259840 | bytes 38014976 | tf_op jit(solution)/shard_map/while/body/eval_jaxpr/qhd,khd->hqk/dot_general | solution.py:32
  138.2 14.1 %fusion.35 = f32[2,512]{1,0:T(2,128)S(1)} fusion(f32[2,512,8192]{2,1,0:T(8,128)} %get-tuple-element.85, f32[2,512]{1,0:T(2,128)S(1)} %get-tuple-element.86), kind=kLoop, calls=%fused_computation.2.clone.1 | loop fusion | flops 25164800 | bytes 33562624 | tf_op jit(solution)/shard_map/while/body/eval_jaxpr/reduce_sum | solution.py:35
  152.3 15.1 %fusion.36 = bf16[512,2,128]{0,2,1:T(8,128)(2,1)S(1)} fusion(bf16[8192,2,128]{0,2,1:T(8,128)(2,1)} %get-tuple-element.103, f32[2,512,8192]{2,1,0:T(8,128)} %get-tuple-element.85, f32[2,512]{1,0:T(2,128)S(1)} %get-tuple-element.86, f32[512,2]{0,1:T(2,128)S(1)} %bitcast.68), kind=kOutput, calls=%fused_computation.7.clone.1 | convolution fusion | flops 2172911616 | bytes 38019072 | tf_op jit(solution)/shard_map/while/body/eval_jaxpr/hqk,khd->qhd/dot_general | solution.py:36
  167.5 0.7 constant_dynamic-update-slice_fusion.2
  168.2 87.8 %all-gather.2.cloned.1.call-done = bf16[1024,4096]{1,0:T(8,128)(2,1)} async-done(((bf16[1024,256]{1,0:T(8,128)(2,1)}), bf16[1024,4096]{1,0:T(8,128)(2,1)}) %all-gather.2.cloned.1.call-update) | async-done | bytes 8388624 | tf_op jit(solution)/shard_map/all_gather | solution.py:61
  256.0 6.3 %fusion.17 = bf16[1024,320]{0,1:T(8,128)(2,1)S(1)} fusion(bf16[1024,4096]{1,0:T(8,128)(2,1)} %all-gather.2.cloned.1.call-done, bf16[1,4096,320]{1,2,0:T(8,128)(2,1)S(1)} %copy-done), kind=kOutput, calls=%fused_computation.18 | convolution fusion | flops 2684682240 | bytes 11665408 | tf_op jit(solution)/shard_map/dot_general | solution.py:62
  262.3 1.2 copy.33
  263.5 4.7 %all-to-all-start.3 = ((bf16[16,64,320]{2,1,0:T(8,128)(2,1)}), bf16[16,64,320]{2,1,0:T(8,128)(2,1)S(1)}, u32[]{:S(2)}, u32[]{:S(2)}) async-start(bf16[16,64,320]{2,1,0:T(8,128)(2,1)} %bitcast.63), calls=%async_computation.3 | async-start | bytes 1572864 | tf_op jit(solution)/shard_map/all_to_all | solution.py:63
  268.2 12.4 %all-to-all-done.3 = bf16[16,64,320]{2,1,0:T(8,128)(2,1)S(1)} async-done(((bf16[16,64,320]{2,1,0:T(8,128)(2,1)}), bf16[16,64,320]{2,1,0:T(8,128)(2,1)S(1)}, u32[]{:S(2)}, u32[]{:S(2)}) %all-to-all-start.3) | async-done | bytes 655392 | tf_op jit(solution)/shard_map/all_to_all | solution.py:63
  280.6 0.1 convert_bitcast_fusion
  280.7 2.1 copy.34
  282.8 2.7 reshape.47
  285.5 1.6 fusion.20
  287.1 0.8 constant_dynamic-slice_fusion.1
  287.8 2.8 collective-permute-start.1
  290.7 1.3 collective-permute-start
  291.9 0.3 collective-permute-done.1
  292.3 1.9 fusion.23
  294.1 14.7 %collective-permute-done = bf16[64,5120]{1,0:T(8,128)(2,1)S(1)} collective-permute-done((bf16[64,5120]{1,0:T(8,128)(2,1)S(1)}, bf16[64,5120]{1,0:T(8,128)(2,1)S(1)}, u32[]{:S(2)}, u32[]{:S(2)}) %collective-permute-start) | collective-permute-done | bytes 655392 | tf_op jit(solution)/shard_map/ppermute | solution.py:14
  308.8 0.8 copy.57
  (8 shorter events, 0.3 us)
Async XLA Ops:
  7.2 248.9 %copy-start = (bf16[1,4096,320]{1,2,0:T(8,128)(2,1)S(1)}, bf16[1,4096,320]{1,2,0:T(8,128)(2,1)}, u32[]{:S(2)}) copy-start(bf16[1,4096,320]{1,2,0:T(8,128)(2,1)} %param.15) | copy-start | bytes 7864324
  9.4 17.9 %all-to-all-start.1 = ((bf16[64,16,256]{2,0,1:T(8,128)(2,1)}), bf16[64,16,256]{2,0,1:T(8,128)(2,1)S(1)}, u32[]{:S(2)}, u32[]{:S(2)}) async-start(bf16[64,16,256]{2,0,1:T(8,128)(2,1)} %copy.24), calls=%async_computation.1 | async-start | bytes 1048576 | tf_op jit(solution)/shard_map/all_to_all | solution.py:54
  27.3 20.5 %all-to-all-start = ((bf16[64,16,256]{2,0,1:T(8,128)(2,1)}), bf16[64,16,256]{2,0,1:T(8,128)(2,1)}, u32[]{:S(2)}, u32[]{:S(2)}) async-start(bf16[64,16,256]{2,0,1:T(8,128)(2,1)} %copy.23), calls=%async_computation | async-start | bytes 1048576 | tf_op jit(solution)/shard_map/all_to_all | solution.py:52
  47.9 19.6 %all-to-all-start.2 = ((bf16[64,16,256]{2,0,1:T(8,128)(2,1)}), bf16[64,16,256]{2,0,1:T(8,128)(2,1)}, u32[]{:S(2)}, u32[]{:S(2)}) async-start(bf16[64,16,256]{2,0,1:T(8,128)(2,1)} %copy.27), calls=%async_computation.2 | async-start | bytes 1048576 | tf_op jit(solution)/shard_map/all_to_all | solution.py:55
  54.5 201.6 %all-gather.2.cloned.1.call-start = ((), (), s32[]{:S(2)}) async-start(), calls=%async_computation.4 | async-start | bytes 8912896 | tf_op jit(solution)/shard_map/all_gather | solution.py:61
  263.5 17.1 %all-to-all-start.3 = ((bf16[16,64,320]{2,1,0:T(8,128)(2,1)}), bf16[16,64,320]{2,1,0:T(8,128)(2,1)S(1)}, u32[]{:S(2)}, u32[]{:S(2)}) async-start(bf16[16,64,320]{2,1,0:T(8,128)(2,1)} %bitcast.63), calls=%async_computation.3 | async-start | bytes 1572864 | tf_op jit(solution)/shard_map/all_to_all | solution.py:63
  287.8 4.4 %collective-permute-start.1 = (bf16[64,2560]{1,0:T(8,128)(2,1)}, bf16[64,2560]{1,0:T(8,128)(2,1)}, u32[]{:S(2)}, u32[]{:S(2)}) collective-permute-start(bf16[64,2560]{1,0:T(8,128)(2,1)} %constant_dynamic-slice_fusion.1), channel_id=1, source_target_pairs={{0,128},{128,0},{1,129},{129,1},{2,130},{130,2},{3,131},{131,3},{4... | collective-permute-start | bytes 983048 | tf_op jit(solution)/shard_map/ppermute | solution.py:18
  290.7 18.1 %collective-permute-start = (bf16[64,5120]{1,0:T(8,128)(2,1)S(1)}, bf16[64,5120]{1,0:T(8,128)(2,1)S(1)}, u32[]{:S(2)}, u32[]{:S(2)}) collective-permute-start(bf16[64,5120]{1,0:T(8,128)(2,1)S(1)} %fusion.20), channel_id=1, source_target_pairs={{0,16},{16,32},{32,48},{48,64},{64,80},{80,96},{96,112},{112,0},{1... | collective-permute-start | bytes 1966088 | tf_op jit(solution)/shard_map/ppermute | solution.py:14
Sparse Core Ops, SparseCore 0:
  168.4 87.6 all-gather.1
where the time goes:
time: 318 us; the launch traced here: 316 us
  waiting for transfers between devices  123 us (39%)
  matrix products  67.2 us (21%)
  local copies, waits for them, and re-layouts  43.7 us (14%)
  other arithmetic  40.6 us (13%)
  starting transfers between devices  27.4 us (9%)
  between operations  14.2 us (4%)
    all_gather x1, waiting for transfers between devices, on_device(): features = lax.all_gather(attended, 'sp', axis=1, tiled=True)  87.8 us
    dot_general x2, matrix products, one_block(): jnp.einsum('qhd,khd->hqk', q_block, k_heads, preferred_element_type=jnp.f...  30.8 us
    dot_general x2, matrix products, one_block(): jnp.einsum('hqk,khd->qhd', weights.astype(jnp.bfloat16), v_heads, preferr...  30.2 us
    reduce_sum x2, other arithmetic, one_block(): total = jnp.sum(weights, axis=-1)  28.1 us
    unnamed x8, local copies, waits for them, and re-layouts  16.4 us
    ppermute x1, waiting for transfers between devices, from_behind(): lax.ppermute(array, axis, [(i, (i + by) % devices) for i in range(devices)])  14.7 us
    all_to_all x1, waiting for transfers between devices, on_device(): lax.all_to_all(columns.astype(jnp.bfloat16), 'sp', split_axis=0, concat_a...  12.4 us
    all_to_all x1, waiting for transfers between devices, on_device(): lax.all_to_all(k_tokens, 'sp', split_axis=1, concat_axis=0, tiled=True)  8.2 us
  transfers between devices with their start and end apart: 7, of which 5 were waited for; matrix products, arithmetic and copies ran while one was open for 10% of the time, Pallas kernels for 0%

commit v1 on v0

--- a/solution.py
+++ b/solution.py
@@ -1,6 +1,8 @@
 import jax
 import jax.numpy as jnp
 from jax import lax
+from jax.experimental import pallas as pl
+from jax.experimental.pallas import tpu as pltpu
 from jax.sharding import PartitionSpec as P
 
 HEAD_DIM = 128
@@ -18,31 +20,57 @@
     return lax.ppermute(array, axis, [(i, i ^ 1 << bit) for i in range(lax.axis_size(axis))])
 
 
-def attend(query_rows, key_rows, value_rows):
-    count = query_rows.shape[0]
-    heads = query_rows.shape[1] // HEAD_DIM
-    block = min(512, count)
-    scale = 1.0 / HEAD_DIM**0.5
-    q_blocks = query_rows.reshape(count // block, block, heads, HEAD_DIM)
-    k_heads = key_rows.reshape(-1, heads, HEAD_DIM)
-    v_heads = value_rows.reshape(-1, heads, HEAD_DIM)
+SCALE = 1.4426950408889634 / HEAD_DIM**0.5
+Q_BLOCK = 256
+K_BLOCK = 1024
 
-    def one_block(q_block):
-        scores = (
-            jnp.einsum("qhd,khd->hqk", q_block, k_heads, preferred_element_type=jnp.float32) * scale
-        )
-        weights = jnp.exp(scores - jnp.max(scores, axis=-1, keepdims=True))
-        total = jnp.sum(weights, axis=-1)
-        mixed = jnp.einsum(
-            "hqk,khd->qhd",
-            weights.astype(jnp.bfloat16),
-            v_heads,
-            preferred_element_type=jnp.float32,
-        )
-        mixed = mixed / total.T[:, :, None]
-        return mixed.astype(jnp.bfloat16).reshape(block, heads * HEAD_DIM)
 
-    return lax.map(one_block, q_blocks).reshape(count, heads * HEAD_DIM)
+def attend_kernel(q_ref, k_new, v_new, k_old, v_old, o_ref):
+    blocks = 1 + k_old.shape[0] // K_BLOCK
+
+    def one_block(i, carry):
+        rows = pl.ds(pl.multiple_of(i * Q_BLOCK, Q_BLOCK), Q_BLOCK)
+        for h in range(q_ref.shape[1] // HEAD_DIM):
+            cols = slice(h * HEAD_DIM, (h + 1) * HEAD_DIM)
+            scaled = q_ref[rows, cols].astype(jnp.float32) * SCALE
+            high = scaled.astype(jnp.bfloat16)
+            low = (scaled - high.astype(jnp.float32)).astype(jnp.bfloat16)
+            q = jnp.concatenate([high, low], axis=1)
+            top = acc = None
+            for j in range(blocks):
+                if j == 0:
+                    k, v = k_new[:, cols], v_new[:, cols]
+                else:
+                    part = slice((j - 1) * K_BLOCK, j * K_BLOCK)
+                    k, v = k_old[part, cols], v_old[part, cols]
+                s = lax.dot_general(
+                    q,
+                    jnp.concatenate([k, k], axis=1),
+                    (((1,), (1,)), ((), ())),
+                    preferred_element_type=jnp.float32,
+                )
+                here = jnp.max(s, axis=1, keepdims=True)
+                peak = here if top is None else jnp.maximum(top, here)
+                w = jnp.exp2(s - peak).astype(jnp.bfloat16)
+                both = jnp.concatenate([v, jnp.ones_like(v)], axis=1)
+                r = jnp.dot(w, both, preferred_element_type=jnp.float32)
+                acc = r if top is None else acc * jnp.exp2(top - peak) + r
+                top = peak
+            out = acc[:, :HEAD_DIM] / acc[:, HEAD_DIM:]
+            o_ref[rows, cols] = out.astype(jnp.bfloat16)
+        return carry
+
+    lax.fori_loop(0, q_ref.shape[0] // Q_BLOCK, one_block, 0)
+
+
+def attend(q, k_new, v_new, k_old, v_old):
+    return pl.pallas_call(
+        attend_kernel,
+        out_shape=jax.ShapeDtypeStruct(q.shape, jnp.bfloat16),
+        in_specs=[pl.BlockSpec(memory_space=pltpu.VMEM)] * 5,
+        out_specs=pl.BlockSpec(memory_space=pltpu.VMEM),
+        compiler_params=pltpu.CompilerParams(vmem_limit_bytes=48 * 2**20),
+    )(q, k_new, v_new, k_old, v_old)
 
 
 def on_device(hidden, query, key_new, value_new, stale_key, stale_value, out_weight):
@@ -54,9 +82,7 @@
         lax.all_to_all(k_tokens, "sp", split_axis=1, concat_axis=0, tiled=True),
         lax.all_to_all(v_tokens, "sp", split_axis=1, concat_axis=0, tiled=True),
     )
-    keys = jnp.concatenate([k_all, stale_key[0, 0]], axis=0)
-    values = jnp.concatenate([v_all, stale_value[0, 0]], axis=0)
-    attended = attend(q_all, keys, values)
+    attended = attend(q_all, k_all, v_all, stale_key[0, 0], stale_value[0, 0])
     weight = out_weight[0]
     features = lax.all_gather(attended, "sp", axis=1, tiled=True)
     columns = jnp.dot(features, weight, preferred_element_type=jnp.float32)

time: 318 us -> 226 us (0.71)
  matrix products: 67.2 us -> 6.27 us
  other arithmetic: 40.6 us -> 3.61 us
  local copies, waits for them, and re-layouts: 43.7 us -> 16.8 us
  Pallas kernels: 0 us -> 22.6 us
  blocking collectives: 0 us -> 12.5 us
  starting transfers between devices: 27.4 us -> 20.7 us
  waiting for transfers between devices: 123 us -> 128 us
    dot_general x4 -> x0, matrix products: 60.9 us -> none  [the longest x2 30.8 us: one_block(): jnp.einsum('qhd,khd->hqk', q_block, k_heads, preferred_element_type=jnp.f...]
    reduce_sum x2 -> x0, other arithmetic: 28.1 us -> none  [one_block(): total = jnp.sum(weights, axis=-1)]
    pallas_call x0 -> x1, Pallas kernels: none -> 22.6 us  [attend(): pl.pallas_call(attend_kernel, out_shape=jax.ShapeDtypeStruct(q.shape, jnp...]
    all_to_all x0 -> x1, blocking collectives: none -> 12.5 us  [on_device(): lax.all_to_all(v_tokens, 'sp', split_axis=1, concat_axis=0, tiled=True)]
    unnamed x8 -> x10, local copies, waits for them, and re-layouts: 16.4 us -> 7.26 us
    concatenate x2 -> x0, other arithmetic: 8.83 us -> none  [the longest x1 4.41 us: on_device(): keys = jnp.concatenate([k_all, stale_key[0, 0]], axis=0)]
    all_to_all x1, waiting for transfers between devices: 0.01 us -> 8.2 us  [on_device(): lax.all_to_all(q_tokens, 'sp', split_axis=1, concat_axis=0, tiled=True)]
    all_to_all x1 -> x0, starting transfers between devices: 6.59 us -> none  [on_device(): lax.all_to_all(v_tokens, 'sp', split_axis=1, concat_axis=0, tiled=True)]
  transfers between devices with their start and end apart: 7 -> 6, of which waited for: 5 -> 6; matrix products, arithmetic and copies ran while one was open for 10% -> 3% of each run, Pallas kernels for 0% -> 0%
where the time goes in v1:
time: 226 us; the launch traced here: 225 us
  waiting for transfers between devices  128 us (57%)
  Pallas kernels  22.6 us (10%)
  starting transfers between devices  20.7 us (9%)
  local copies, waits for them, and re-layouts  16.8 us (7%)
  between operations  14.1 us (6%)
  blocking collectives  12.5 us (6%)
  matrix products  6.27 us (3%)
  other arithmetic  3.61 us (2%)
    all_gather x1, waiting for transfers between devices, on_device(): features = lax.all_gather(attended, 'sp', axis=1, tiled=True)  85.8 us
    pallas_call x1, Pallas kernels, attend(): pl.pallas_call(attend_kernel, out_shape=jax.ShapeDtypeStruct(q.shape, jnp...  22.6 us
    ppermute x1, waiting for transfers between devices, from_behind(): lax.ppermute(array, axis, [(i, (i + by) % devices) for i in range(devices)])  14.7 us
    all_to_all x1, blocking collectives, on_device(): lax.all_to_all(v_tokens, 'sp', split_axis=1, concat_axis=0, tiled=True)  12.5 us
    all_to_all x1, waiting for transfers between devices, on_device(): lax.all_to_all(columns.astype(jnp.bfloat16), 'sp', split_axis=0, concat_a...  12.4 us
    all_to_all x1, waiting for transfers between devices, on_device(): lax.all_to_all(q_tokens, 'sp', split_axis=1, concat_axis=0, tiled=True)  8.2 us
    all_to_all x1, starting transfers between devices, on_device(): lax.all_to_all(q_tokens, 'sp', split_axis=1, concat_axis=0, tiled=True)  7.58 us
    unnamed x10, local copies, waits for them, and re-layouts  7.26 us
  transfers between devices with their start and end apart: 6, of which 6 were waited for; matrix products, arithmetic and copies ran while one was open for 3% of the time, Pallas kernels for 0%

profile of v1, /device:TPU:1, one launch (start us, length us, event | category | flops | bytes accessed | tf_op | source)
XLA Modules:
  0.0 225.0 jit_solution(11404297722533852658)
XLA Ops:
  7.2 0.0 copy-start
  7.2 1.3 copy.22
  8.5 1.0 copy.17
  9.4 7.6 %all-to-all-start = ((bf16[64,16,256]{2,0,1:T(8,128)(2,1)}), bf16[64,16,256]{2,0,1:T(8,128)(2,1)S(1)}, u32[]{:S(2)}, u32[]{:S(2)}) async-start(bf16[64,16,256]{2,0,1:T(8,128)(2,1)} %copy.17), calls=%async_computation | async-start | bytes 1048576 | tf_op jit(solution)/shard_map/all_to_all | solution.py:80
  17.0 1.1 copy.23
  18.2 1.0 copy.18
  19.1 8.2 %all-to-all-done = bf16[64,16,256]{2,0,1:T(8,128)(2,1)S(1)} async-done(((bf16[64,16,256]{2,0,1:T(8,128)(2,1)}), bf16[64,16,256]{2,0,1:T(8,128)(2,1)S(1)}, u32[]{:S(2)}, u32[]{:S(2)}) %all-to-all-start) | async-done | bytes 524320 | tf_op jit(solution)/shard_map/all_to_all | solution.py:80
  27.3 4.2 %all-to-all-start.1 = ((bf16[64,16,256]{2,0,1:T(8,128)(2,1)}), bf16[64,16,256]{2,0,1:T(8,128)(2,1)}, u32[]{:S(2)}, u32[]{:S(2)}) async-start(bf16[64,16,256]{2,0,1:T(8,128)(2,1)} %copy.18), calls=%async_computation.1 | async-start | bytes 1048576 | tf_op jit(solution)/shard_map/all_to_all | solution.py:82
  31.6 0.0 all-gather.2.cloned.1.call-start
  31.6 1.1 copy.24
  32.8 1.0 copy.19
  33.7 7.0 %all-to-all-done.1 = bf16[64,16,256]{2,0,1:T(8,128)(2,1)} async-done(((bf16[64,16,256]{2,0,1:T(8,128)(2,1)}), bf16[64,16,256]{2,0,1:T(8,128)(2,1)}, u32[]{:S(2)}, u32[]{:S(2)}) %all-to-all-start.1) | async-done | bytes 524320 | tf_op jit(solution)/shard_map/all_to_all | solution.py:82
  40.8 12.5 %all_to_all.70 = bf16[64,16,256]{2,0,1:T(8,128)(2,1)S(1)} all-to-all(bf16[64,16,256]{2,0,1:T(8,128)(2,1)} %copy.19), channel_id=1, replica_groups=mesh['cfg'=2,'pipe'=8,'sp'=16] {'sp'}, dimensions={1} | all-to-all | bytes 1048576 | tf_op jit(solution)/shard_map/all_to_all | solution.py:83
  53.2 0.0 copy-start.1
  53.2 2.0 copy-done.1
  55.3 22.6 %shard_map.86 = bf16[1024,256]{1,0:T(8,128)(2,1)S(1)} custom-call(bf16[1024,256]{1,0:T(8,128)(2,1)S(1)} %bitcast.39, bf16[1024,256]{1,0:T(8,128)(2,1)} %bitcast.4.k_new, bf16[1024,256]{1,0:T(8,128)(2,1)S(1)} %bitcast.40, bf16[7168,256]{1,0:T(8,128)(2,1)S(1)} %bitcast.38, bf16[7168,256]{1,0:T(8,128)(2,1)} %bitcast.41), custom_call_target="tpu_custom_call" | custom-call | tf_op jit(solution)/shard_map/pallas_call | solution.py:67
  77.9 0.0 copy-start.2
  77.9 0.8 copy-done.2
  78.7 0.0 all-gather.2.cloned.1.call-update
  78.8 85.8 %all-gather.2.cloned.1.call-done = bf16[1024,4096]{1,0:T(8,128)(2,1)} async-done(((bf16[1024,256]{1,0:T(8,128)(2,1)}), bf16[1024,4096]{1,0:T(8,128)(2,1)}) %all-gather.2.cloned.1.call-update) | async-done | bytes 8388624 | tf_op jit(solution)/shard_map/all_gather | solution.py:87
  164.5 0.0 copy-done
  164.5 6.3 %fusion.2 = bf16[1024,320]{0,1:T(8,128)(2,1)S(1)} fusion(bf16[1024,4096]{1,0:T(8,128)(2,1)} %all-gather.2.cloned.1.call-done, bf16[1,4096,320]{1,2,0:T(8,128)(2,1)S(1)} %copy-done), kind=kOutput, calls=%fused_computation.3 | convolution fusion | flops 2684682240 | bytes 11665408 | tf_op jit(solution)/shard_map/dot_general | solution.py:88
  170.8 1.2 copy.20
  172.0 4.7 %all-to-all-start.3 = ((bf16[16,64,320]{2,1,0:T(8,128)(2,1)}), bf16[16,64,320]{2,1,0:T(8,128)(2,1)S(1)}, u32[]{:S(2)}, u32[]{:S(2)}) async-start(bf16[16,64,320]{2,1,0:T(8,128)(2,1)} %bitcast.42), calls=%async_computation.3 | async-start | bytes 1572864 | tf_op jit(solution)/shard_map/all_to_all | solution.py:89
  176.7 12.4 %all-to-all-done.3 = bf16[16,64,320]{2,1,0:T(8,128)(2,1)S(1)} async-done(((bf16[16,64,320]{2,1,0:T(8,128)(2,1)}), bf16[16,64,320]{2,1,0:T(8,128)(2,1)S(1)}, u32[]{:S(2)}, u32[]{:S(2)}) %all-to-all-start.3) | async-done | bytes 655392 | tf_op jit(solution)/shard_map/all_to_all | solution.py:89
  189.1 0.1 convert_bitcast_fusion
  189.2 2.1 copy.21
  191.3 2.7 %reshape.24 = f32[64,5120]{1,0:T(8,128)} reshape(f32[64,16,320]{2,1,0:T(8,128)} %copy.21) | data formatting | bytes 2621440 | tf_op jit(solution)/shard_map/convert_element_type | solution.py:91
  194.0 1.6 fusion.5
  195.6 0.8 constant_dynamic-slice_fusion
  196.4 2.8 %collective-permute-start.1 = (bf16[64,2560]{1,0:T(8,128)(2,1)}, bf16[64,2560]{1,0:T(8,128)(2,1)}, u32[]{:S(2)}, u32[]{:S(2)}) collective-permute-start(bf16[64,2560]{1,0:T(8,128)(2,1)} %constant_dynamic-slice_fusion), channel_id=1, source_target_pairs={{0,128},{128,0},{1,129},{129,1},{2,130},{130,2},{3,131},{131,3},{4... | collective-permute-start | bytes 983048 | tf_op jit(solution)/shard_map/ppermute | solution.py:20
  199.2 1.3 collective-permute-start
  200.5 0.3 collective-permute-done.1
  200.8 1.9 fusion.8
  202.7 14.7 %collective-permute-done = bf16[64,5120]{1,0:T(8,128)(2,1)S(1)} collective-permute-done((bf16[64,5120]{1,0:T(8,128)(2,1)S(1)}, bf16[64,5120]{1,0:T(8,128)(2,1)S(1)}, u32[]{:S(2)}, u32[]{:S(2)}) %collective-permute-start) | collective-permute-done | bytes 655392 | tf_op jit(solution)/shard_map/ppermute | solution.py:16
  217.4 0.8 copy.26
Async XLA Ops:
  7.2 157.4 %copy-start = (bf16[1,4096,320]{1,2,0:T(8,128)(2,1)S(1)}, bf16[1,4096,320]{1,2,0:T(8,128)(2,1)}, u32[]{:S(2)}) copy-start(bf16[1,4096,320]{1,2,0:T(8,128)(2,1)} %param.13) | copy-start | bytes 7864324
  9.4 17.9 %all-to-all-start = ((bf16[64,16,256]{2,0,1:T(8,128)(2,1)}), bf16[64,16,256]{2,0,1:T(8,128)(2,1)S(1)}, u32[]{:S(2)}, u32[]{:S(2)}) async-start(bf16[64,16,256]{2,0,1:T(8,128)(2,1)} %copy.17), calls=%async_computation | async-start | bytes 1048576 | tf_op jit(solution)/shard_map/all_to_all | solution.py:80
  27.3 13.4 %all-to-all-start.1 = ((bf16[64,16,256]{2,0,1:T(8,128)(2,1)}), bf16[64,16,256]{2,0,1:T(8,128)(2,1)}, u32[]{:S(2)}, u32[]{:S(2)}) async-start(bf16[64,16,256]{2,0,1:T(8,128)(2,1)} %copy.18), calls=%async_computation.1 | async-start | bytes 1048576 | tf_op jit(solution)/shard_map/all_to_all | solution.py:82
  31.6 132.9 %all-gather.2.cloned.1.call-start = ((), (), s32[]{:S(2)}) async-start(), calls=%async_computation.4 | async-start | bytes 8912896 | tf_op jit(solution)/shard_map/all_gather | solution.py:87
  53.2 2.0 copy-start.1
  77.9 0.8 copy-start.2
  172.0 17.1 %all-to-all-start.3 = ((bf16[16,64,320]{2,1,0:T(8,128)(2,1)}), bf16[16,64,320]{2,1,0:T(8,128)(2,1)S(1)}, u32[]{:S(2)}, u32[]{:S(2)}) async-start(bf16[16,64,320]{2,1,0:T(8,128)(2,1)} %bitcast.42), calls=%async_computation.3 | async-start | bytes 1572864 | tf_op jit(solution)/shard_map/all_to_all | solution.py:89
  196.4 4.4 %collective-permute-start.1 = (bf16[64,2560]{1,0:T(8,128)(2,1)}, bf16[64,2560]{1,0:T(8,128)(2,1)}, u32[]{:S(2)}, u32[]{:S(2)}) collective-permute-start(bf16[64,2560]{1,0:T(8,128)(2,1)} %constant_dynamic-slice_fusion), channel_id=1, source_target_pairs={{0,128},{128,0},{1,129},{129,1},{2,130},{130,2},{3,131},{131,3},{4... | collective-permute-start | bytes 983048 | tf_op jit(solution)/shard_map/ppermute | solution.py:20
  199.2 18.1 %collective-permute-start = (bf16[64,5120]{1,0:T(8,128)(2,1)S(1)}, bf16[64,5120]{1,0:T(8,128)(2,1)S(1)}, u32[]{:S(2)}, u32[]{:S(2)}) collective-permute-start(bf16[64,5120]{1,0:T(8,128)(2,1)S(1)} %fusion.5), channel_id=1, source_target_pairs={{0,16},{16,32},{32,48},{48,64},{64,80},{80,96},{96,112},{112,0},{1... | collective-permute-start | bytes 1966088 | tf_op jit(solution)/shard_map/ppermute | solution.py:16
Sparse Core Ops, SparseCore 0:
  78.9 85.5 all-gather.1

commit v2 on v0

v2 whole, which is shorter than its diff:
```python
import functools

import jax
import jax.numpy as jnp
from jax import lax
from jax.experimental import pallas as pl
from jax.experimental.pallas import tpu as pltpu
from jax.sharding import PartitionSpec as P

HEAD_DIM = 128
SCALE = 1.4426950408889634 / HEAD_DIM**0.5
GUIDANCE = 5.0
MESH = pl.DeviceIdType.MESH
SIDE = 4
PEERS = SIDE * SIDE
BLOCKS = 4
OWN = 16
ROWS = PEERS * OWN
FEAT = 256
WIDE = SIDE * FEAT
SLICE = 320
COLS = SIDE * SLICE
MODEL = PEERS * SLICE
HALF = MODEL // 2
FRESH = 1024
STALE = 7168
K_BLOCK = 1024


def remote(src, dst, send, recv, **to):
    return pltpu.make_async_remote_copy(src, dst, send, recv, device_id=to, device_id_type=MESH)


def attend_part(q, k_ref, v_ref, starts, cols, top, acc):
    for start in starts:
        part = pl.ds(start, K_BLOCK)
        k, v = k_ref[part, cols], v_ref[part, cols]
        s = lax.dot_general(
            q,
            jnp.concatenate([k, k], axis=1),
            (((1,), (1,)), ((), ())),
            preferred_element_type=jnp.float32,
        )
        here = jnp.max(s, axis=1, keepdims=True)
        peak = here if top is None else jnp.maximum(top, here)
        w = jnp.exp2(s - peak).astype(jnp.bfloat16)
        both = jnp.concatenate([v, jnp.ones_like(v)], axis=1)
        r = jnp.dot(w, both, preferred_element_type=jnp.float32)
        acc = r if top is None else acc * jnp.exp2(top - peak) + r
        top = peak
    return top, acc


def kernel(
    hid_in, q_in, k_in, v_in, k_old, v_old, w_in,
    next_out, guided_out,
    qs, ks, vs, tops, accs, feat, wr, ws, part, rs, rsum, fin, hid, bo, gx, gd,
    q_s, q_r, k_s, k_r, v_s, v_r, w_s, w_r, wx_s, wx_r,
    ag_s, ag_r, rs_s, rs_r, fin_s, fin_r, z_s, z_r, g_s, g_r, loc, out_sem,
):
    me = lax.axis_index("sp")
    core = lax.axis_index("cfg")
    sec = lax.axis_index("pipe")
    sections = lax.axis_size("pipe")
    x, y = lax.div(me, SIDE), lax.rem(me, SIDE)
    behind = lax.rem(sec + 1, sections)
    before = lax.rem(sec + sections - 1, sections)

    def peer(n):
        return lax.rem(me + n, PEERS)

    def x_peer(d):
        return lax.rem(x + d, SIDE)

    def y_peer(d):
        return lax.rem(y + d, SIDE)

    old = pl.ds(FRESH, STALE)
    locals_ = [
        pltpu.make_async_copy(k_old, ks.at[old], loc.at[0]),
        pltpu.make_async_copy(v_old, vs.at[old], loc.at[1]),
        pltpu.make_async_copy(q_in.at[:, :, pl.ds(pl.multiple_of(me * FEAT, FEAT), FEAT)], qs.at[:, me], loc.at[2]),
        pltpu.make_async_copy(k_in.at[:, pl.ds(pl.multiple_of(me * FEAT, FEAT), FEAT)], ks.at[pl.ds(pl.multiple_of(me * 64, 64), 64)], loc.at[3]),
        pltpu.make_async_copy(v_in.at[:, pl.ds(pl.multiple_of(me * FEAT, FEAT), FEAT)], vs.at[pl.ds(pl.multiple_of(me * 64, 64), 64)], loc.at[4]),
        pltpu.make_async_copy(w_in.at[pl.ds(pl.multiple_of(x * WIDE, WIDE), WIDE)], wr.at[x], loc.at[5]),
        pltpu.make_async_copy(hid_in, hid, loc.at[6]),
    ]

    def q_copy(n):
        to = peer(n)
        return remote(q_in.at[:, :, pl.ds(pl.multiple_of(to * FEAT, FEAT), FEAT)], qs.at[:, me], q_s.at[n - 1], q_r.at[n - 1], sp=to)

    def k_copy(n):
        to = peer(n)
        return remote(k_in.at[:, pl.ds(pl.multiple_of(to * FEAT, FEAT), FEAT)], ks.at[pl.ds(pl.multiple_of(me * 64, 64), 64)], k_s.at[n - 1], k_r.at[n - 1], sp=to)

    def v_copy(n):
        to = peer(n)
        return remote(v_in.at[:, pl.ds(pl.multiple_of(to * FEAT, FEAT), FEAT)], vs.at[pl.ds(pl.multiple_of(me * 64, 64), 64)], v_s.at[n - 1], v_r.at[n - 1], sp=to)

    half = pl.ds(pl.multiple_of(core * (WIDE // 2), WIDE // 2), WIDE // 2)

    def w_copy(d):
        to = x_peer(d)
        rows = pl.ds(pl.multiple_of(to * WIDE + core * (WIDE // 2), WIDE // 2), WIDE // 2)
        return remote(w_in.at[rows], wr.at[x, half], w_s.at[d - 1], w_r.at[d - 1], sp=to * SIDE + y)

    def w_cross(d):
        source = x_peer(SIDE - d)
        return remote(wr.at[source, half], wr.at[source, half], wx_s.at[d - 1], wx_r.at[d - 1], cfg=1 - core)

    def ag_copy(b, d):
        return remote(feat.at[b, y], feat.at[b, y], ag_s.at[b, d - 1], ag_r.at[b, d - 1], sp=x * SIDE + y_peer(d))

    def rs_copy(b, d):
        to = x_peer(d)
        rows = pl.ds(pl.multiple_of(to * 64, 64), 64)
        return remote(part.at[b, rows], rs.at[b, d - 1], rs_s.at[b, d - 1], rs_r.at[b, d - 1], sp=to * SIDE + y)

    def fin_copy(b, d):
        to = y_peer(d)
        return remote(rsum.at[b, to], fin.at[b, y], fin_s.at[b, d - 1], fin_r.at[b, d - 1], sp=x * SIDE + to)

    def z_copy(b):
        return remote(bo.at[b], next_out.at[b], z_s.at[b], z_r.at[b], pipe=behind)

    def g_copy(b):
        theirs = pl.ds(pl.multiple_of((1 - core) * HALF, HALF), HALF)
        return remote(bo.at[b, :, theirs], gx.at[b], g_s.at[b], g_r.at[b], cfg=1 - core)

    def each(low, high, act):
        def step(n, carry):
            act(n)
            return carry

        lax.fori_loop(low, high, step, 0)

    for copy in locals_:
        copy.start()

    barrier = pltpu.get_barrier_semaphore()
    each(1, PEERS, lambda n: pl.semaphore_signal(barrier, inc=1, device_id={"sp": peer(n)}, device_id_type=MESH))
    pl.semaphore_signal(barrier, inc=1, device_id={"cfg": 1 - core}, device_id_type=MESH)
    pl.semaphore_signal(barrier, inc=1, device_id={"pipe": behind}, device_id_type=MESH)
    pl.semaphore_signal(barrier, inc=1, device_id={"pipe": before}, device_id_type=MESH)
    pl.semaphore_wait(barrier, PEERS + 2)

    each(1, PEERS, lambda n: q_copy(n).start())
    for copy in locals_:
        copy.wait()
    each(1, PEERS, lambda n: q_copy(n).wait_recv())

    def send_kv(n):
        k_copy(n).start()
        v_copy(n).start()

    each(1, PEERS, send_kv)

    def queries(b, cols):
        scaled = qs[b, :, :, cols].reshape(ROWS, HEAD_DIM).astype(jnp.float32) * SCALE
        high = scaled.astype(jnp.bfloat16)
        low = (scaled - high.astype(jnp.float32)).astype(jnp.bfloat16)
        return jnp.concatenate([high, low], axis=1)

    def stale(b):
        for h in range(2):
            cols = slice(h * HEAD_DIM, (h + 1) * HEAD_DIM)
            top, acc = attend_part(queries(b, cols), ks, vs, range(FRESH, FRESH + STALE, K_BLOCK), cols, None, None)
            tops[b, h] = jnp.broadcast_to(top, (ROWS, HEAD_DIM))
            accs[b, h] = acc

    def fresh(b):
        for h in range(2):
            cols = slice(h * HEAD_DIM, (h + 1) * HEAD_DIM)
            top, acc = attend_part(queries(b, cols), ks, vs, [0], cols, tops[b, h][:, :1], accs[b, h])
            out = acc[:, :HEAD_DIM] / acc[:, HEAD_DIM:]
            feat[b, y, :, cols] = out.astype(jnp.bfloat16)
        each(1, SIDE, lambda d: ag_copy(b, d).start())

    def weights():
        each(1, SIDE, lambda d: w_cross(d).wait_recv())
        chunk = 128

        def lay(i, carry):
            rows = pl.ds(pl.multiple_of(i * chunk, chunk), chunk)
            for s in range(SIDE):
                ws[rows, s * SLICE : (s + 1) * SLICE] = wr[s, rows]
            return carry

        lax.fori_loop(0, WIDE // chunk, lay, 0)

    def project(b):
        each(1, SIDE, lambda d: ag_copy(b, d).wait_recv())
        a = jnp.concatenate([feat[b, i] for i in range(SIDE)], axis=1)
        for n in range(0, COLS, 256):
            r = jnp.dot(a, ws[:, n : n + 256], preferred_element_type=jnp.float32)
            part[b, :, n : n + 256] = r.astype(jnp.bfloat16)
        each(1, SIDE, lambda d: rs_copy(b, d).start())

    def reduce(b):
        each(1, SIDE, lambda d: rs_copy(b, d).wait_recv())
        total = part[b, pl.ds(pl.multiple_of(x * 64, 64), 64)].astype(jnp.float32)
        for d in range(SIDE - 1):
            total = total + rs[b, d].astype(jnp.float32)
        rsum[b] = total.astype(jnp.bfloat16).reshape(SIDE, OWN, COLS)
        fin[b, y] = rsum[b, y]
        each(1, SIDE, lambda d: fin_copy(b, d).start())

    def finish(b):
        each(1, SIDE, lambda d: fin_copy(b, d).wait_recv())
        for s in range(SIDE):
            proj = jnp.concatenate([fin[b, i, :, s * SLICE : (s + 1) * SLICE] for i in range(SIDE)], axis=1)
            wide = slice(s * COLS, (s + 1) * COLS)
            bo[b, :, wide] = (hid[b, :, wide].astype(jnp.float32) + proj.astype(jnp.float32)).astype(jnp.bfloat16)
        z_copy(b).start()
        g_copy(b).start()

    def guide(b):
        g_copy(b).wait_recv()
        own = bo[b, :, pl.ds(pl.multiple_of(core * HALF, HALF), HALF)].astype(jnp.float32)
        other = gx[b].astype(jnp.float32)
        first = core == 0
        cond = jnp.where(first, own, other)
        uncond = jnp.where(first, other, own)
        gd[b] = (uncond + GUIDANCE * (cond - uncond)).astype(jnp.bfloat16)
        pltpu.make_async_copy(gd.at[b], guided_out.at[b], out_sem.at[b]).start()

    def step(t, carry):
        @pl.when(t < BLOCKS)
        def _():
            stale(t)

        @pl.when(t == 0)
        def _():
            each(1, SIDE, lambda d: w_copy(d).start())

        @pl.when(t == 1)
        def _():
            def got(n):
                k_copy(n).wait_recv()
                v_copy(n).wait_recv()

            each(1, PEERS, got)
            fresh(0)

        @pl.when((t >= 1) & (t < BLOCKS))
        def _():
            fresh(t)

        @pl.when(t == 2)
        def _():
            def cross(d):
                w_copy(d).wait_recv()
                w_cross(d).start()

            each(1, SIDE, cross)
            weights()

        @pl.when((t >= 2) & (t < BLOCKS + 2))
        def _():
            project(t - 2)

        @pl.when((t >= 3) & (t < BLOCKS + 3))
        def _():
            reduce(t - 3)

        @pl.when((t >= 4) & (t < BLOCKS + 4))
        def _():
            finish(t - 4)

        @pl.when(t >= 5)
        def _():
            guide(t - 5)

        return carry

    lax.fori_loop(0, BLOCKS + 5, step, 0)

    def sent(n):
        q_copy(n).wait_send()
        k_copy(n).wait_send()
        v_copy(n).wait_send()

    each(1, PEERS, sent)

    def sent_w(d):
        w_copy(d).wait_send()
        w_cross(d).wait_send()

    each(1, SIDE, sent_w)

    def sent_block(b):
        def sent_peer(d):
            ag_copy(b, d).wait_send()
            rs_copy(b, d).wait_send()
            fin_copy(b, d).wait_send()

        each(1, SIDE, sent_peer)
        z_copy(b).wait()
        g_copy(b).wait_send()
        pltpu.make_async_copy(gd.at[b], guided_out.at[b], out_sem.at[b]).wait()

    each(0, BLOCKS, sent_block)


def on_device(hidden, query, key_new, value_new, stale_key, stale_value, out_weight):
    bf16, f32 = jnp.bfloat16, jnp.float32
    vmem, dma = pltpu.VMEM, pltpu.SemaphoreType.DMA
    handed, guided = pl.pallas_call(
        kernel,
        out_shape=(
            jax.ShapeDtypeStruct((BLOCKS, OWN, MODEL), bf16),
            jax.ShapeDtypeStruct((BLOCKS, OWN, HALF), bf16),
        ),
        in_specs=[pl.BlockSpec(memory_space=pl.ANY)] * 7,
        out_specs=(pl.BlockSpec(memory_space=pl.ANY),) * 2,
        scratch_shapes=[
            vmem((BLOCKS, PEERS, OWN, FEAT), bf16),
            vmem((FRESH + STALE, FEAT), bf16),
            vmem((FRESH + STALE, FEAT), bf16),
            vmem((BLOCKS, 2, ROWS, HEAD_DIM), f32),
            vmem((BLOCKS, 2, ROWS, 2 * HEAD_DIM), f32),
            vmem((BLOCKS, SIDE, ROWS, FEAT), bf16),
            vmem((SIDE, WIDE, SLICE), bf16),
            vmem((WIDE, COLS), bf16),
            vmem((BLOCKS, ROWS, COLS), bf16),
            vmem((BLOCKS, SIDE - 1, 64, COLS), bf16),
            vmem((BLOCKS, SIDE, OWN, COLS), bf16),
            vmem((BLOCKS, SIDE, OWN, COLS), bf16),
            vmem((BLOCKS, OWN, MODEL), bf16),
            vmem((BLOCKS, OWN, MODEL), bf16),
            vmem((BLOCKS, OWN, HALF), bf16),
            vmem((BLOCKS, OWN, HALF), bf16),
        ]
        + [dma((PEERS - 1,))] * 6
        + [dma((SIDE - 1,))] * 4
        + [dma((BLOCKS, SIDE - 1))] * 6
        + [dma((BLOCKS,))] * 4
        + [dma((7,)), dma((BLOCKS,))],
        compiler_params=pltpu.CompilerParams(collective_id=0, has_side_effects=True, vmem_limit_bytes=56 * 2**20),
    )(
        hidden.reshape(BLOCKS, OWN, MODEL),
        query.reshape(BLOCKS, OWN, PEERS * FEAT),
        key_new[0, 0],
        value_new[0, 0],
        stale_key[0, 0],
        stale_value[0, 0],
        out_weight[0],
    )
    return (handed.reshape(1, 1, BLOCKS * OWN, MODEL), guided.reshape(1, BLOCKS * OWN, HALF))


def solution(mesh):
    return jax.shard_map(
        on_device,
        mesh=mesh,
        in_specs=(
            P("cfg", "pipe", "sp", None),
            P("cfg", "pipe", "sp", None),
            P("cfg", "pipe", "sp", None),
            P("cfg", "pipe", "sp", None),
            P("cfg", "pipe", None, "sp"),
            P("cfg", "pipe", None, "sp"),
            P("pipe", None, "sp"),
        ),
        out_specs=(P("cfg", "pipe", "sp", None), P("pipe", "sp", "cfg")),
        check_vma=False,
    )
```

time: 318 us -> 106 us (0.33)
  waiting for transfers between devices: 123 us -> 0 us
  Pallas kernels: 0 us -> 96.5 us
  matrix products: 67.2 us -> 0 us
  other arithmetic: 40.6 us -> 0 us
  local copies, waits for them, and re-layouts: 43.7 us -> 8.24 us
  starting transfers between devices: 27.4 us -> 0 us
  between operations: 14.2 us -> 0.64 us
    pallas_call x0 -> x1, Pallas kernels: none -> 96.5 us  [on_device(): pl.pallas_call(kernel, out_shape=(jax.ShapeDtypeStruct((BLOCKS, OWN, MODE...]
    all_gather x1 -> x0, waiting for transfers between devices: 87.8 us -> none  [on_device(): features = lax.all_gather(attended, 'sp', axis=1, tiled=True)]
    dot_general x5 -> x0, matrix products: 67.2 us -> none  [the longest x2 30.8 us: one_block(): jnp.einsum('qhd,khd->hqk', q_block, k_heads, preferred_element_type=jnp.f...]
    reduce_sum x2 -> x0, other arithmetic: 28.1 us -> none  [one_block(): total = jnp.sum(weights, axis=-1)]
    all_to_all x4 -> x0, starting transfers between devices: 23.1 us -> none  [the longest x1 7.58 us: on_device(): lax.all_to_all(k_tokens, 'sp', split_axis=1, concat_axis=0, tiled=True)]
    all_to_all x4 -> x0, waiting for transfers between devices: 20.6 us -> none  [the longest x1 12.4 us: on_device(): lax.all_to_all(columns.astype(jnp.bfloat16), 'sp', split_axis=0, concat_a...]
    ppermute x2 -> x0, waiting for transfers between devices: 15 us -> none  [the longest x1 14.7 us: from_behind(): lax.ppermute(array, axis, [(i, (i + by) % devices) for i in range(devices)])]
    concatenate x2 -> x0, other arithmetic: 8.83 us -> none  [the longest x1 4.41 us: on_device(): keys = jnp.concatenate([k_all, stale_key[0, 0]], axis=0)]
  transfers between devices with their start and end apart: 7 -> 0, of which waited for: 5 -> 0; matrix products, arithmetic and copies ran while one was open for 10% -> 0% of each run, Pallas kernels for 0% -> 0%
where the time goes in v2:
time: 106 us; the launch traced here: 105 us
  Pallas kernels  96.5 us (91%)
  local copies, waits for them, and re-layouts  8.24 us (8%)
    pallas_call x1, Pallas kernels, on_device(): pl.pallas_call(kernel, out_shape=(jax.ShapeDtypeStruct((BLOCKS, OWN, MODE...  96.5 us
    unnamed x3, local copies, waits for them, and re-layouts  8.24 us

profile of v2, /device:TPU:1, one launch (start us, length us, event | category | flops | bytes accessed | tf_op | source)
XLA Modules:
  0.0 105.3 jit_solution(12955458901059803)
XLA Ops:
  0.6 4.6 %copy.9 = bf16[1,4096,320]{2,1,0:T(8,128)(2,1)} copy(bf16[1,4096,320]{1,2,0:T(8,128)(2,1)} %param.13) | data formatting | bytes 5242880 | tf_op args[6]
  5.2 96.5 %shard_map.86 = (bf16[4,16,5120]{2,1,0:T(8,128)(2,1)}, bf16[4,16,2560]{2,1,0:T(8,128)(2,1)}) custom-call(bf16[4,16,5120]{2,1,0:T(8,128)(2,1)} %bitcast.12, bf16[4,16,4096]{2,1,0:T(8,128)(2,1)} %bitcast.14, bf16[64,4096]{1,0:T(8,128)(2,1)} %bitcast.15, bf16[64,4096]{1,0:T(8,128)(2,1)} %bitcast.16, bf16[7168,256]{1,0:T(8,128)(2,1)} %bitcast.10, ...), custom_call_target="tpu_custom_call" | custom-call | tf_op jit(solution)/shard_map/pallas_call | solution.py:309
  101.7 2.0 %copy.12 = bf16[1,1,64,5120]{3,2,1,0:T(8,128)(2,1)} copy(bf16[1,1,64,5120]{3,2,1,0:T(8,128)(2,1)} %bitcast.13) | data formatting | bytes 1310720
  103.6 1.7 %copy.13 = bf16[1,64,2560]{2,1,0:T(8,128)(2,1)} copy(bf16[1,64,2560]{2,1,0:T(8,128)(2,1)} %bitcast.17) | data formatting | bytes 655360

commit v3 on v2

--- a/solution.py
+++ b/solution.py
@@ -25,6 +25,9 @@
 FRESH = 1024
 STALE = 7168
 K_BLOCK = 1024
+W_PARTS = 4
+W_AT = 1
+W_ROWS = SLICE // W_PARTS
 
 
 def remote(src, dst, send, recv, **to):
@@ -54,9 +57,9 @@
 def kernel(
     hid_in, q_in, k_in, v_in, k_old, v_old, w_in,
     next_out, guided_out,
-    qs, ks, vs, tops, accs, feat, wr, ws, part, rs, rsum, fin, hid, bo, gx, gd,
+    qs, ks, vs, tops, accs, feat, ws, part, far, near, rsum, fin, hid, bo, gx, gd,
     q_s, q_r, k_s, k_r, v_s, v_r, w_s, w_r, wx_s, wx_r,
-    ag_s, ag_r, rs_s, rs_r, fin_s, fin_r, z_s, z_r, g_s, g_r, loc, out_sem,
+    ag_s, ag_r, far_s, far_r, near_s, near_r, fin_s, fin_r, z_s, z_r, g_s, g_r, loc, out_sem,
 ):
     me = lax.axis_index("sp")
     core = lax.axis_index("cfg")
@@ -82,7 +85,7 @@
         pltpu.make_async_copy(q_in.at[:, :, pl.ds(pl.multiple_of(me * FEAT, FEAT), FEAT)], qs.at[:, me], loc.at[2]),
         pltpu.make_async_copy(k_in.at[:, pl.ds(pl.multiple_of(me * FEAT, FEAT), FEAT)], ks.at[pl.ds(pl.multiple_of(me * 64, 64), 64)], loc.at[3]),
         pltpu.make_async_copy(v_in.at[:, pl.ds(pl.multiple_of(me * FEAT, FEAT), FEAT)], vs.at[pl.ds(pl.multiple_of(me * 64, 64), 64)], loc.at[4]),
-        pltpu.make_async_copy(w_in.at[pl.ds(pl.multiple_of(x * WIDE, WIDE), WIDE)], wr.at[x], loc.at[5]),
+        pltpu.make_async_copy(w_in.at[:, pl.ds(pl.multiple_of(x * WIDE, WIDE), WIDE)], ws.at[x], loc.at[5]),
         pltpu.make_async_copy(hid_in, hid, loc.at[6]),
     ]
 
@@ -100,22 +103,30 @@
 
     half = pl.ds(pl.multiple_of(core * (WIDE // 2), WIDE // 2), WIDE // 2)
 
-    def w_copy(d):
+    def w_copy(p, d):
         to = x_peer(d)
-        rows = pl.ds(pl.multiple_of(to * WIDE + core * (WIDE // 2), WIDE // 2), WIDE // 2)
-        return remote(w_in.at[rows], wr.at[x, half], w_s.at[d - 1], w_r.at[d - 1], sp=to * SIDE + y)
-
-    def w_cross(d):
-        source = x_peer(SIDE - d)
-        return remote(wr.at[source, half], wr.at[source, half], wx_s.at[d - 1], wx_r.at[d - 1], cfg=1 - core)
+        rows = pl.ds(pl.multiple_of(p * W_ROWS, W_ROWS), W_ROWS)
+        cols = pl.ds(pl.multiple_of(to * WIDE + core * (WIDE // 2), WIDE // 2), WIDE // 2)
+        return remote(w_in.at[rows, cols], ws.at[x, rows, half], w_s.at[p, d - 1], w_r.at[p, d - 1], sp=to * SIDE + y)
+
+    def w_cross(p, d):
+        rows = pl.ds(pl.multiple_of(p * W_ROWS, W_ROWS), W_ROWS)
+        piece = ws.at[x_peer(SIDE - d), rows, half]
+        return remote(piece, piece, wx_s.at[p, d - 1], wx_r.at[p, d - 1], cfg=1 - core)
 
     def ag_copy(b, d):
         return remote(feat.at[b, y], feat.at[b, y], ag_s.at[b, d - 1], ag_r.at[b, d - 1], sp=x * SIDE + y_peer(d))
 
-    def rs_copy(b, d):
-        to = x_peer(d)
-        rows = pl.ds(pl.multiple_of(to * 64, 64), 64)
-        return remote(part.at[b, rows], rs.at[b, d - 1], rs_s.at[b, d - 1], rs_r.at[b, d - 1], sp=to * SIDE + y)
+    def rows_of(to, start, size):
+        return pl.ds(pl.multiple_of(to * 64 + start, size), size)
+
+    def far_copy(b, way):
+        rows = rows_of(x_peer(2), 32 * way, 32)
+        return remote(part.at[b, rows], far.at[b, way], far_s.at[b, way], far_r.at[b, way], sp=x_peer(1 + 2 * way) * SIDE + y)
+
+    def near_copy(b, way):
+        to = x_peer(1 + 2 * way)
+        return remote(part.at[b, rows_of(to, 0, 64)], near.at[b, way], near_s.at[b, way], near_r.at[b, way], sp=to * SIDE + y)
 
     def fin_copy(b, d):
         to = y_peer(d)
@@ -177,31 +188,31 @@
             feat[b, y, :, cols] = out.astype(jnp.bfloat16)
         each(1, SIDE, lambda d: ag_copy(b, d).start())
 
-    def weights():
-        each(1, SIDE, lambda d: w_cross(d).wait_recv())
-        chunk = 128
-
-        def lay(i, carry):
-            rows = pl.ds(pl.multiple_of(i * chunk, chunk), chunk)
-            for s in range(SIDE):
-                ws[rows, s * SLICE : (s + 1) * SLICE] = wr[s, rows]
-            return carry
-
-        lax.fori_loop(0, WIDE // chunk, lay, 0)
-
     def project(b):
         each(1, SIDE, lambda d: ag_copy(b, d).wait_recv())
         a = jnp.concatenate([feat[b, i] for i in range(SIDE)], axis=1)
+        w = ws[...].reshape(COLS, WIDE)
         for n in range(0, COLS, 256):
-            r = jnp.dot(a, ws[:, n : n + 256], preferred_element_type=jnp.float32)
+            r = lax.dot_general(
+                a, w[n : n + 256], (((1,), (1,)), ((), ())), preferred_element_type=jnp.float32
+            )
             part[b, :, n : n + 256] = r.astype(jnp.bfloat16)
-        each(1, SIDE, lambda d: rs_copy(b, d).start())
+        far_copy(b, 0).start()
+        far_copy(b, 1).start()
+
+    def merge(b):
+        for way in range(2):
+            far_copy(b, way).wait_recv()
+            rows = rows_of(x_peer(1 + 2 * way), 32 * way, 32)
+            both = part[b, rows].astype(jnp.float32) + far[b, way].astype(jnp.float32)
+            part[b, rows] = both.astype(jnp.bfloat16)
+            near_copy(b, way).start()
 
     def reduce(b):
-        each(1, SIDE, lambda d: rs_copy(b, d).wait_recv())
-        total = part[b, pl.ds(pl.multiple_of(x * 64, 64), 64)].astype(jnp.float32)
-        for d in range(SIDE - 1):
-            total = total + rs[b, d].astype(jnp.float32)
+        total = part[b, rows_of(x, 0, 64)].astype(jnp.float32)
+        for way in range(2):
+            near_copy(b, way).wait_recv()
+            total = total + near[b, way].astype(jnp.float32)
         rsum[b] = total.astype(jnp.bfloat16).reshape(SIDE, OWN, COLS)
         fin[b, y] = rsum[b, y]
         each(1, SIDE, lambda d: fin_copy(b, d).start())
@@ -225,77 +236,71 @@
         gd[b] = (uncond + GUIDANCE * (cond - uncond)).astype(jnp.bfloat16)
         pltpu.make_async_copy(gd.at[b], guided_out.at[b], out_sem.at[b]).start()
 
-    def step(t, carry):
-        @pl.when(t < BLOCKS)
-        def _():
-            stale(t)
-
-        @pl.when(t == 0)
-        def _():
-            each(1, SIDE, lambda d: w_copy(d).start())
-
-        @pl.when(t == 1)
-        def _():
-            def got(n):
-                k_copy(n).wait_recv()
-                v_copy(n).wait_recv()
-
-            each(1, PEERS, got)
-            fresh(0)
-
-        @pl.when((t >= 1) & (t < BLOCKS))
-        def _():
-            fresh(t)
-
-        @pl.when(t == 2)
-        def _():
-            def cross(d):
-                w_copy(d).wait_recv()
-                w_cross(d).start()
-
-            each(1, SIDE, cross)
-            weights()
-
-        @pl.when((t >= 2) & (t < BLOCKS + 2))
-        def _():
-            project(t - 2)
-
-        @pl.when((t >= 3) & (t < BLOCKS + 3))
-        def _():
-            reduce(t - 3)
-
-        @pl.when((t >= 4) & (t < BLOCKS + 4))
-        def _():
-            finish(t - 4)
-
-        @pl.when(t >= 5)
-        def _():
-            guide(t - 5)
-
-        return carry
-
-    lax.fori_loop(0, BLOCKS + 5, step, 0)
+    def got(n):
+        k_copy(n).wait_recv()
+        v_copy(n).wait_recv()
 
     def sent(n):
         q_copy(n).wait_send()
         k_copy(n).wait_send()
         v_copy(n).wait_send()
 
+    def parts(act):
+        each(0, W_PARTS, lambda p: each(1, SIDE, lambda d: act(p, d)))
+
+    def cross(p, d):
+        w_copy(p, d).wait_recv()
+        w_cross(p, d).start()
+
+    def attend(b, carry):
+        stale(b)
+
+        @pl.when(b == W_AT)
+        def _():
+            parts(lambda p, d: w_copy(p, d).start())
+
+        @pl.when(b == 1)
+        def _():
+            each(1, PEERS, got)
+            fresh(0)
+
+        @pl.when(b >= 1)
+        def _():
+            fresh(b)
+
+        return carry
+
+    lax.fori_loop(0, BLOCKS, attend, 0)
     each(1, PEERS, sent)
-
-    def sent_w(d):
-        w_copy(d).wait_send()
-        w_cross(d).wait_send()
-
-    each(1, SIDE, sent_w)
+    parts(cross)
+    parts(lambda p, d: w_cross(p, d).wait_recv())
+
+    def step(t, carry):
+        for lag, act in enumerate((project, merge, reduce, finish, guide)):
+
+            @pl.when((t >= lag) & (t < BLOCKS + lag))
+            def _():
+                act(t - lag)
+
+        return carry
+
+    lax.fori_loop(0, BLOCKS + 4, step, 0)
+
+    def sent_w(p, d):
+        w_copy(p, d).wait_send()
+        w_cross(p, d).wait_send()
+
+    parts(sent_w)
 
     def sent_block(b):
         def sent_peer(d):
             ag_copy(b, d).wait_send()
-            rs_copy(b, d).wait_send()
             fin_copy(b, d).wait_send()
 
         each(1, SIDE, sent_peer)
+        for way in range(2):
+            far_copy(b, way).wait_send()
+            near_copy(b, way).wait_send()
         z_copy(b).wait()
         g_copy(b).wait_send()
         pltpu.make_async_copy(gd.at[b], guided_out.at[b], out_sem.at[b]).wait()
@@ -321,10 +326,10 @@
             vmem((BLOCKS, 2, ROWS, HEAD_DIM), f32),
             vmem((BLOCKS, 2, ROWS, 2 * HEAD_DIM), f32),
             vmem((BLOCKS, SIDE, ROWS, FEAT), bf16),
-            vmem((SIDE, WIDE, SLICE), bf16),
-            vmem((WIDE, COLS), bf16),
+            vmem((SIDE, SLICE, WIDE), bf16),
             vmem((BLOCKS, ROWS, COLS), bf16),
-            vmem((BLOCKS, SIDE - 1, 64, COLS), bf16),
+            vmem((BLOCKS, 2, 32, COLS), bf16),
+            vmem((BLOCKS, 2, 64, COLS), bf16),
             vmem((BLOCKS, SIDE, OWN, COLS), bf16),
             vmem((BLOCKS, SIDE, OWN, COLS), bf16),
             vmem((BLOCKS, OWN, MODEL), bf16),
@@ -333,8 +338,10 @@
             vmem((BLOCKS, OWN, HALF), bf16),
         ]
         + [dma((PEERS - 1,))] * 6
-        + [dma((SIDE - 1,))] * 4
-        + [dma((BLOCKS, SIDE - 1))] * 6
+        + [dma((W_PARTS, SIDE - 1))] * 4
+        + [dma((BLOCKS, SIDE - 1))] * 2
+        + [dma((BLOCKS, 2))] * 4
+        + [dma((BLOCKS, SIDE - 1))] * 2
         + [dma((BLOCKS,))] * 4
         + [dma((7,)), dma((BLOCKS,))],
         compiler_params=pltpu.CompilerParams(collective_id=0, has_side_effects=True, vmem_limit_bytes=56 * 2**20),
@@ -345,7 +352,7 @@
         value_new[0, 0],
         stale_key[0, 0],
         stale_value[0, 0],
-        out_weight[0],
+        out_weight[0].T,
     )
     return (handed.reshape(1, 1, BLOCKS * OWN, MODEL), guided.reshape(1, BLOCKS * OWN, HALF))
 

time: 106 us -> 93.3 us (0.88)
  Pallas kernels: 96.5 us -> 88.8 us
  local copies, waits for them, and re-layouts: 8.24 us -> 3.68 us
    pallas_call x1, Pallas kernels: 96.5 us -> 88.8 us  [on_device(): pl.pallas_call(kernel, out_shape=(jax.ShapeDtypeStruct((BLOCKS, OWN, MODE...]
    unnamed x3 -> x2, local copies, waits for them, and re-layouts: 8.24 us -> 3.68 us
where the time goes in v3:
time: 93.3 us; the launch traced here: 93.1 us
  Pallas kernels  88.8 us (95%)
  local copies, waits for them, and re-layouts  3.68 us (4%)
    pallas_call x1, Pallas kernels, on_device(): pl.pallas_call(kernel, out_shape=(jax.ShapeDtypeStruct((BLOCKS, OWN, MODE...  88.8 us
    unnamed x2, local copies, waits for them, and re-layouts  3.68 us

profile of v3, /device:TPU:1, one launch (start us, length us, event | category | flops | bytes accessed | tf_op | source)
XLA Modules:
  0.0 93.1 jit_solution(3233825160129076068)
XLA Ops:
  0.6 88.8 %shard_map.86 = (bf16[4,16,5120]{2,1,0:T(8,128)(2,1)}, bf16[4,16,2560]{2,1,0:T(8,128)(2,1)}) custom-call(bf16[4,16,5120]{2,1,0:T(8,128)(2,1)} %bitcast.14, bf16[4,16,4096]{2,1,0:T(8,128)(2,1)} %bitcast.16, bf16[64,4096]{1,0:T(8,128)(2,1)} %bitcast.17, bf16[64,4096]{1,0:T(8,128)(2,1)} %bitcast.18, bf16[7168,256]{1,0:T(8,128)(2,1)} %bitcast.11, ...), custom_call_target="tpu_custom_call" | custom-call | tf_op jit(solution)/shard_map/pallas_call | solution.py:314
  89.4 2.0 %copy.11 = bf16[1,1,64,5120]{3,2,1,0:T(8,128)(2,1)} copy(bf16[1,1,64,5120]{3,2,1,0:T(8,128)(2,1)} %bitcast.15) | data formatting | bytes 1310720
  91.4 1.7 %copy.12 = bf16[1,64,2560]{2,1,0:T(8,128)(2,1)} copy(bf16[1,64,2560]{2,1,0:T(8,128)(2,1)} %bitcast.19) | data formatting | bytes 655360

commit v4 on v3

--- a/solution.py
+++ b/solution.py
@@ -26,8 +26,11 @@
 STALE = 7168
 K_BLOCK = 1024
 W_PARTS = 4
-W_AT = 1
 W_ROWS = SLICE // W_PARTS
+PARTS = 2
+PAIR = SIDE // PARTS
+PCOLS = PAIR * SLICE
+UNITS = PARTS * BLOCKS
 
 
 def remote(src, dst, send, recv, **to):
@@ -120,24 +123,30 @@
     def rows_of(to, start, size):
         return pl.ds(pl.multiple_of(to * 64 + start, size), size)
 
-    def far_copy(b, way):
+    def far_copy(p, b, way):
         rows = rows_of(x_peer(2), 32 * way, 32)
-        return remote(part.at[b, rows], far.at[b, way], far_s.at[b, way], far_r.at[b, way], sp=x_peer(1 + 2 * way) * SIDE + y)
-
-    def near_copy(b, way):
+        to = x_peer(1 + 2 * way) * SIDE + y
+        return remote(part.at[p, b, rows], far.at[p, b, way], far_s.at[p, b, way], far_r.at[p, b, way], sp=to)
+
+    def near_copy(p, b, way):
         to = x_peer(1 + 2 * way)
-        return remote(part.at[b, rows_of(to, 0, 64)], near.at[b, way], near_s.at[b, way], near_r.at[b, way], sp=to * SIDE + y)
-
-    def fin_copy(b, d):
+        rows = rows_of(to, 0, 64)
+        return remote(part.at[p, b, rows], near.at[p, b, way], near_s.at[p, b, way], near_r.at[p, b, way], sp=to * SIDE + y)
+
+    def fin_copy(p, b, d):
         to = y_peer(d)
-        return remote(rsum.at[b, to], fin.at[b, y], fin_s.at[b, d - 1], fin_r.at[b, d - 1], sp=x * SIDE + to)
-
-    def z_copy(b):
-        return remote(bo.at[b], next_out.at[b], z_s.at[b], z_r.at[b], pipe=behind)
+        return remote(rsum.at[p, b, to], fin.at[p, b, y], fin_s.at[p, b, d - 1], fin_r.at[p, b, d - 1], sp=x * SIDE + to)
+
+    def z_copy(p, b):
+        cols = pl.ds(pl.multiple_of(p * HALF, HALF), HALF)
+        return remote(bo.at[b, :, cols], next_out.at[b, :, cols], z_s.at[p, b], z_r.at[p, b], pipe=behind)
 
     def g_copy(b):
         theirs = pl.ds(pl.multiple_of((1 - core) * HALF, HALF), HALF)
         return remote(bo.at[b, :, theirs], gx.at[b], g_s.at[b], g_r.at[b], cfg=1 - core)
+
+    def guided_copy(b):
+        return pltpu.make_async_copy(gd.at[b], guided_out.at[b], out_sem.at[b])
 
     def each(low, high, act):
         def step(n, carry):
@@ -188,43 +197,45 @@
             feat[b, y, :, cols] = out.astype(jnp.bfloat16)
         each(1, SIDE, lambda d: ag_copy(b, d).start())
 
-    def project(b):
-        each(1, SIDE, lambda d: ag_copy(b, d).wait_recv())
+    def project(p, b):
         a = jnp.concatenate([feat[b, i] for i in range(SIDE)], axis=1)
-        w = ws[...].reshape(COLS, WIDE)
-        for n in range(0, COLS, 256):
-            r = lax.dot_general(
-                a, w[n : n + 256], (((1,), (1,)), ((), ())), preferred_element_type=jnp.float32
-            )
-            part[b, :, n : n + 256] = r.astype(jnp.bfloat16)
-        far_copy(b, 0).start()
-        far_copy(b, 1).start()
-
-    def merge(b):
+        w = ws[pl.ds(p * PAIR, PAIR)].reshape(PCOLS, WIDE)
+        for n in range(0, PCOLS, 256):
+            cols = slice(n, min(n + 256, PCOLS))
+            r = lax.dot_general(a, w[cols], (((1,), (1,)), ((), ())), preferred_element_type=jnp.float32)
+            part[p, b, :, cols] = r.astype(jnp.bfloat16)
+        far_copy(p, b, 0).start()
+        far_copy(p, b, 1).start()
+
+    def merge(p, b):
         for way in range(2):
-            far_copy(b, way).wait_recv()
+            far_copy(p, b, way).wait_recv()
             rows = rows_of(x_peer(1 + 2 * way), 32 * way, 32)
-            both = part[b, rows].astype(jnp.float32) + far[b, way].astype(jnp.float32)
-            part[b, rows] = both.astype(jnp.bfloat16)
-            near_copy(b, way).start()
-
-    def reduce(b):
-        total = part[b, rows_of(x, 0, 64)].astype(jnp.float32)
+            both = part[p, b, rows].astype(jnp.float32) + far[p, b, way].astype(jnp.float32)
+            part[p, b, rows] = both.astype(jnp.bfloat16)
+            near_copy(p, b, way).start()
+
+    def reduce(p, b):
+        total = part[p, b, rows_of(x, 0, 64)].astype(jnp.float32)
         for way in range(2):
-            near_copy(b, way).wait_recv()
-            total = total + near[b, way].astype(jnp.float32)
-        rsum[b] = total.astype(jnp.bfloat16).reshape(SIDE, OWN, COLS)
-        fin[b, y] = rsum[b, y]
-        each(1, SIDE, lambda d: fin_copy(b, d).start())
-
-    def finish(b):
-        each(1, SIDE, lambda d: fin_copy(b, d).wait_recv())
-        for s in range(SIDE):
-            proj = jnp.concatenate([fin[b, i, :, s * SLICE : (s + 1) * SLICE] for i in range(SIDE)], axis=1)
-            wide = slice(s * COLS, (s + 1) * COLS)
+            near_copy(p, b, way).wait_recv()
+            total = total + near[p, b, way].astype(jnp.float32)
+        rsum[p, b] = total.astype(jnp.bfloat16).reshape(SIDE, OWN, PCOLS)
+        fin[p, b, y] = rsum[p, b, y]
+        each(1, SIDE, lambda d: fin_copy(p, b, d).start())
+
+    def finish(p, b):
+        each(1, SIDE, lambda d: fin_copy(p, b, d).wait_recv())
+        for s in range(PAIR):
+            cols = slice(s * SLICE, (s + 1) * SLICE)
+            proj = jnp.concatenate([fin[p, b, i, :, cols] for i in range(SIDE)], axis=1)
+            wide = pl.ds(pl.multiple_of((p * PAIR + s) * COLS, COLS), COLS)
             bo[b, :, wide] = (hid[b, :, wide].astype(jnp.float32) + proj.astype(jnp.float32)).astype(jnp.bfloat16)
-        z_copy(b).start()
-        g_copy(b).start()
+        z_copy(p, b).start()
+
+        @pl.when(p == 1 - core)
+        def _():
+            g_copy(b).start()
 
     def guide(b):
         g_copy(b).wait_recv()
@@ -234,7 +245,7 @@
         cond = jnp.where(first, own, other)
         uncond = jnp.where(first, other, own)
         gd[b] = (uncond + GUIDANCE * (cond - uncond)).astype(jnp.bfloat16)
-        pltpu.make_async_copy(gd.at[b], guided_out.at[b], out_sem.at[b]).start()
+        guided_copy(b).start()
 
     def got(n):
         k_copy(n).wait_recv()
@@ -255,13 +266,10 @@
     def attend(b, carry):
         stale(b)
 
-        @pl.when(b == W_AT)
-        def _():
+        @pl.when(b == 1)
+        def _():
+            each(1, PEERS, got)
             parts(lambda p, d: w_copy(p, d).start())
-
-        @pl.when(b == 1)
-        def _():
-            each(1, PEERS, got)
             fresh(0)
 
         @pl.when(b >= 1)
@@ -271,39 +279,55 @@
         return carry
 
     lax.fori_loop(0, BLOCKS, attend, 0)
-    each(1, PEERS, sent)
     parts(cross)
     parts(lambda p, d: w_cross(p, d).wait_recv())
-
-    def step(t, carry):
-        for lag, act in enumerate((project, merge, reduce, finish, guide)):
-
-            @pl.when((t >= lag) & (t < BLOCKS + lag))
-            def _():
-                act(t - lag)
-
-        return carry
-
-    lax.fori_loop(0, BLOCKS + 4, step, 0)
 
     def sent_w(p, d):
         w_copy(p, d).wait_send()
         w_cross(p, d).wait_send()
 
-    parts(sent_w)
+    def settle(p, b):
+        for way in range(2):
+            far_copy(p, b, way).wait_send()
+            near_copy(p, b, way).wait_send()
+        each(1, SIDE, lambda d: fin_copy(p, b, d).wait_send())
+
+        @pl.when(p == 0)
+        def _():
+            each(1, SIDE, lambda d: ag_copy(b, d).wait_send())
+
+    def step(t, carry):
+        @pl.when(t == 4)
+        def _():
+            each(1, PEERS, sent)
+
+        @pl.when(t == 5)
+        def _():
+            parts(sent_w)
+
+        @pl.when((t < UNITS) & (lax.rem(t, PARTS) == 0))
+        def _():
+            b = lax.div(t, PARTS)
+            each(1, SIDE, lambda d: ag_copy(b, d).wait_recv())
+
+        for lag, act in ((0, project), (2, merge), (4, reduce), (6, finish), (7, settle)):
+
+            @pl.when((t >= lag) & (t < UNITS + lag))
+            def _():
+                act(lax.rem(t - lag, PARTS), lax.div(t - lag, PARTS))
+
+        @pl.when((t >= 8) & (lax.rem(t - 7, PARTS) == 1))
+        def _():
+            guide(lax.div(t - 7, PARTS))
+
+        return carry
+
+    lax.fori_loop(0, UNITS + 7, step, 0)
 
     def sent_block(b):
-        def sent_peer(d):
-            ag_copy(b, d).wait_send()
-            fin_copy(b, d).wait_send()
-
-        each(1, SIDE, sent_peer)
-        for way in range(2):
-            far_copy(b, way).wait_send()
-            near_copy(b, way).wait_send()
-        z_copy(b).wait()
+        each(0, PARTS, lambda p: z_copy(p, b).wait())
         g_copy(b).wait_send()
-        pltpu.make_async_copy(gd.at[b], guided_out.at[b], out_sem.at[b]).wait()
+        guided_copy(b).wait()
 
     each(0, BLOCKS, sent_block)
 
@@ -327,11 +351,11 @@
             vmem((BLOCKS, 2, ROWS, 2 * HEAD_DIM), f32),
             vmem((BLOCKS, SIDE, ROWS, FEAT), bf16),
             vmem((SIDE, SLICE, WIDE), bf16),
-            vmem((BLOCKS, ROWS, COLS), bf16),
-            vmem((BLOCKS, 2, 32, COLS), bf16),
-            vmem((BLOCKS, 2, 64, COLS), bf16),
-            vmem((BLOCKS, SIDE, OWN, COLS), bf16),
-            vmem((BLOCKS, SIDE, OWN, COLS), bf16),
+            vmem((PARTS, BLOCKS, ROWS, PCOLS), bf16),
+            vmem((PARTS, BLOCKS, 2, 32, PCOLS), bf16),
+            vmem((PARTS, BLOCKS, 2, 64, PCOLS), bf16),
+            vmem((PARTS, BLOCKS, SIDE, OWN, PCOLS), bf16),
+            vmem((PARTS, BLOCKS, SIDE, OWN, PCOLS), bf16),
             vmem((BLOCKS, OWN, MODEL), bf16),
             vmem((BLOCKS, OWN, MODEL), bf16),
             vmem((BLOCKS, OWN, HALF), bf16),
@@ -340,9 +364,10 @@
         + [dma((PEERS - 1,))] * 6
         + [dma((W_PARTS, SIDE - 1))] * 4
         + [dma((BLOCKS, SIDE - 1))] * 2
-        + [dma((BLOCKS, 2))] * 4
-        + [dma((BLOCKS, SIDE - 1))] * 2
-        + [dma((BLOCKS,))] * 4
+        + [dma((PARTS, BLOCKS, 2))] * 4
+        + [dma((PARTS, BLOCKS, SIDE - 1))] * 2
+        + [dma((PARTS, BLOCKS))] * 2
+        + [dma((BLOCKS,))] * 2
         + [dma((7,)), dma((BLOCKS,))],
         compiler_params=pltpu.CompilerParams(collective_id=0, has_side_effects=True, vmem_limit_bytes=56 * 2**20),
     )(

time: 93.3 us -> 90.8 us (0.973)
  Pallas kernels: 88.8 us -> 86.3 us
    pallas_call x1, Pallas kernels: 88.8 us -> 86.3 us  [on_device(): pl.pallas_call(kernel, out_shape=(jax.ShapeDtypeStruct((BLOCKS, OWN, MODE...]
where the time goes in v4:
time: 90.8 us; the launch traced here: 90.7 us
  Pallas kernels  86.3 us (95%)
  local copies, waits for them, and re-layouts  3.68 us (4%)
    pallas_call x1, Pallas kernels, on_device(): pl.pallas_call(kernel, out_shape=(jax.ShapeDtypeStruct((BLOCKS, OWN, MODE...  86.3 us
    unnamed x2, local copies, waits for them, and re-layouts  3.68 us

profile of v4, /device:TPU:1, one launch (start us, length us, event | category | flops | bytes accessed | tf_op | source)
XLA Modules:
  0.0 90.7 jit_solution(17595194509057920097)
XLA Ops:
  0.6 86.3 %shard_map.86 = (bf16[4,16,5120]{2,1,0:T(8,128)(2,1)}, bf16[4,16,2560]{2,1,0:T(8,128)(2,1)}) custom-call(bf16[4,16,5120]{2,1,0:T(8,128)(2,1)} %bitcast.14, bf16[4,16,4096]{2,1,0:T(8,128)(2,1)} %bitcast.16, bf16[64,4096]{1,0:T(8,128)(2,1)} %bitcast.17, bf16[64,4096]{1,0:T(8,128)(2,1)} %bitcast.18, bf16[7168,256]{1,0:T(8,128)(2,1)} %bitcast.11, ...), custom_call_target="tpu_custom_call" | custom-call | tf_op jit(solution)/shard_map/pallas_call | solution.py:338
  87.0 2.0 %copy.11 = bf16[1,1,64,5120]{3,2,1,0:T(8,128)(2,1)} copy(bf16[1,1,64,5120]{3,2,1,0:T(8,128)(2,1)} %bitcast.15) | data formatting | bytes 1310720
  88.9 1.7 %copy.12 = bf16[1,64,2560]{2,1,0:T(8,128)(2,1)} copy(bf16[1,64,2560]{2,1,0:T(8,128)(2,1)} %bitcast.19) | data formatting | bytes 655360
